TPU v7x, 32 devices: a whole 2x2x4 slice. The times are simulated.
32 devices in a mesh: seq: 16 (over z, y, core), tp: 2 (over x).
Axes of the slice: x: 2, y: 2, z: 4, core: 2. Of those that a mesh axis runs over, the one named last changes fastest.
Arguments:
- query_proj: bfloat16 [4096, 3072], P('seq', 'tp'), may hold values from -8 to 8
- key_proj: bfloat16 [4096, 3072], P('seq', 'tp'), may hold values from -8 to 8
- value_proj: bfloat16 [4096, 3072], P('seq', 'tp'), may hold values from -6 to 6
- hidden: bfloat16 [4096, 3072], P('seq', 'tp'), may hold values from -2 to 2
- out_weight: bfloat16 [3072, 3072], P('tp'), may hold values from -0.109375 to 0.109375
- norm_gain: bfloat16 [3072], P('tp'), may hold values from 0.099609375 to 1.8984375
- segment_ids: int32 [4096], P('seq'), may hold values from 0 to 7, never falling along the last dimension, each value on 1 to 2048 neighbouring positions
- pad_mask: int32 [4096], P('seq'), may hold values 0 or 1
- page_table: int32 [32], P('seq'), may hold values from 0 to 1, as said below
Outputs:
- hidden_out: bfloat16 [4096, 3072], P('seq', 'tp')
- normed: bfloat16 [4096, 3072], P('seq', 'tp')
- kv_pages: bfloat16 [32, 2, 128, 3072], P('seq', None, None, 'tp')
Inputs may be any that keep to these rules, and one draw needn't show every extreme that they name: `segment_ids`: never falling along the tokens; each of the 8 prompts has 1 to 2048 tokens, one exactly 2048. `page_table`: the 2 pages of each aligned block of 2 pages name each slot once.
All inputs are finite; a program needn't handle non-finite values. No bound on the sum of `pad_mask` on one device may be relied on, other than what follows from the above.
Results may differ from a plain program's by a relative error of at most 0.014.
Values may be sent and summed in bfloat16 or wider, within the bound.
A program may use at most 128 MiB of HBM per device.

v0:
```python
import math

import jax
import jax.numpy as jnp
from jax import lax
from jax.sharding import PartitionSpec as P

D = 3072
HEAD_DIM = 96
PAGE = 128


far_index = 1073741824
masked_score = -1e30
norm_epsilon = 1e-05


def passed_along(block, axis, distance):
    devices = range(lax.axis_size(axis))
    route = [(i - distance, i) for i in devices if i - distance in devices]
    return lax.ppermute(block, axis, route)


def rotate(values_in, position, head_count, head_dim):
    count_rows = values_in.shape[0]
    half_dim = head_dim // 2
    frequency = jnp.exp(
        jnp.arange(half_dim, dtype=jnp.float32) * (-2.0 * math.log(10000.0) / head_dim)
    )
    angles = position.astype(jnp.float32)[:, None] * frequency[None, :]
    cosine = jnp.cos(angles)[:, None, :]
    sine_part = jnp.sin(angles)[:, None, :]
    as_float = values_in.astype(jnp.float32).reshape(count_rows, head_count, head_dim)
    lower_half = as_float[..., :half_dim]
    upper_half = as_float[..., half_dim:]
    rotated = jnp.concatenate(
        [
            lower_half * cosine - upper_half * sine_part,
            upper_half * cosine + lower_half * sine_part,
        ],
        axis=-1,
    )
    return rotated.reshape(count_rows, head_count * head_dim).astype(jnp.bfloat16)


def attend(softmax_state, query_heads, block, visible):
    row_peak, row_total, weighted = softmax_state
    key_count = block.shape[1]
    head_count = query_heads.shape[1]
    key_heads = block[0].reshape(key_count, head_count, HEAD_DIM)
    val_heads = block[1].reshape(key_count, head_count, HEAD_DIM)
    factor = 1.0 / math.sqrt(HEAD_DIM)
    logits = (
        jnp.einsum("qhd,khd->hqk", query_heads, key_heads, preferred_element_type=jnp.float32)
        * factor
    )
    logits = jnp.where(visible[None], logits, masked_score)
    new_peak = jnp.maximum(row_peak, jnp.max(logits, axis=-1))
    rescale = jnp.exp(row_peak - new_peak)
    unnormed = jnp.where(visible[None], jnp.exp(logits - new_peak[..., None]), 0.0)
    row_total = row_total * rescale + jnp.sum(unnormed, axis=-1)
    weighted = weighted * rescale[..., None] + jnp.einsum(
        "hqk,khd->hqd", unnormed.astype(jnp.bfloat16), val_heads, preferred_element_type=jnp.float32
    )
    return (new_peak, row_total, weighted)


def per_device(
    query_proj,
    key_proj,
    value_proj,
    hidden,
    out_weight,
    norm_gain,
    segment_ids,
    pad_mask,
    page_table,
):
    tok_count = query_proj.shape[0]
    feat_count = query_proj.shape[1]
    head_count = feat_count // HEAD_DIM
    seg_count = lax.axis_size("seq") // 2
    reach_count = lax.axis_size("seq") // 2
    device_row = lax.axis_index("seq")
    tok_index = device_row * tok_count + jnp.arange(tok_count, dtype=jnp.int32)
    member = segment_ids[:, None] == jnp.arange(seg_count, dtype=jnp.int32)[None, :]
    local_first = jnp.min(jnp.where(member, tok_index[:, None], far_index), axis=0)
    first_tok = lax.pmin(local_first, "seq")
    position = tok_index - jnp.sum(jnp.where(member, first_tok[None, :], 0), axis=1)
    q_rot = rotate(query_proj, position, head_count, HEAD_DIM)
    k_rot = rotate(key_proj, position, head_count, HEAD_DIM)
    query_heads = q_rot.reshape(tok_count, head_count, HEAD_DIM)
    query_tag = segment_ids + 1
    key_tag = jnp.where(pad_mask == 1, segment_ids + 1, 0)
    own_block = jnp.stack([k_rot, value_proj])
    offsets = jnp.arange(tok_count, dtype=jnp.int32)
    own_visible = (key_tag[None, :] == query_tag[:, None]) & (
        offsets[None, :] <= offsets[:, None]
    ) | (offsets[None, :] == offsets[:, None])
    softmax_state = (
        jnp.full((head_count, tok_count), masked_score, jnp.float32),
        jnp.zeros((head_count, tok_count), jnp.float32),
        jnp.zeros((head_count, tok_count, HEAD_DIM), jnp.float32),
    )
    softmax_state = attend(softmax_state, query_heads, own_block, own_visible)

    def visit_block(current, moved, moved_tags):
        visible = moved_tags[None, :] == query_tag[:, None]
        return attend(current, query_heads, moved, visible)

    def cycle_turn(turn_index, loop_state):
        current, moved, moved_tags = loop_state
        moved, moved_tags = passed_along((moved, moved_tags), "seq", 1)
        return (visit_block(current, moved, moved_tags), moved, moved_tags)

    softmax_state = lax.fori_loop(0, reach_count, cycle_turn, (softmax_state, own_block, key_tag))[
        0
    ]
    row_peak, row_total, weighted = softmax_state
    attn = (
        jnp.transpose(weighted / row_total[..., None], (1, 0, 2))
        .reshape(tok_count, feat_count)
        .astype(jnp.bfloat16)
    )
    partial_value = jnp.dot(attn, out_weight, preferred_element_type=jnp.float32)
    feature_width = hidden.shape[1]
    summed = lax.psum(partial_value.astype(jnp.bfloat16), "tp").astype(jnp.float32)
    own_sum = lax.dynamic_slice_in_dim(
        summed, lax.axis_index("tp") * feature_width, feature_width, 1
    )
    hidden_out = (hidden.astype(jnp.float32) + own_sum).astype(jnp.bfloat16)
    stream_wide = hidden_out.astype(jnp.float32)
    square_total = lax.psum(jnp.sum(stream_wide * stream_wide, axis=1), "tp")
    normed = (
        stream_wide
        * lax.rsqrt(square_total / D + norm_epsilon)[:, None]
        * norm_gain.astype(jnp.float32)[None, :]
    ).astype(jnp.bfloat16)
    pad_scale = pad_mask.astype(jnp.bfloat16)[:, None]
    page_count = tok_count // PAGE
    stacked = jnp.stack([k_rot * pad_scale, value_proj * pad_scale])
    stacked = stacked.reshape(2, page_count, PAGE, feat_count).transpose(1, 0, 2, 3)
    kv_pages = jnp.zeros_like(stacked).at[page_table].set(stacked)
    return (hidden_out, normed, kv_pages)


def solution(mesh):
    placed = (
        P("seq", "tp"),
        P("seq", "tp"),
        P("seq", "tp"),
        P("seq", "tp"),
        P("tp", None),
        P("tp"),
        P("seq"),
        P("seq"),
        P("seq"),
    )
    return jax.shard_map(
        per_device,
        mesh=mesh,
        in_specs=placed,
        out_specs=(P("seq", "tp"), P("seq", "tp"), P("seq", None, None, "tp")),
        check_vma=False,
    )
```

profile of v0, /device:TPU:16, one launch (start us, length us, event | category | flops | bytes accessed | tf_op | source)
XLA Modules:
  0.0 334.6 jit_solution(4713208961190621794)
XLA Ops:
  8.0 10.1 %pmin.7 = s32[8]{0:T(128)S(1)} all-reduce(s32[8]{0:T(128)S(1)} %select_reduce_fusion.1), channel_id=1, replica_groups=mesh['seq'=16,'tp'=2] {'seq'}, use_global_device_ids=true, to_apply=%region_1.2 | all-reduce | flops 8 | bytes 64 | tf_op jit(solution)/shard_map/pmin | solution.py:88
  26.3 4.5 %fusion.28 = f32[16,256,96]{1,2,0:T(8,128)} fusion(bf16[256,16,96]{0,2,1:T(8,128)(2,1)S(1)} %bitcast.40, f32[16,256,256]{1,2,0:T(8,128)} %copy-done.1, f32[16,256]{1,0:T(8,128)S(1)} %broadcast_maximum_fusion, pred[256,256]{0,1:T(8,128)(4,1)S(1)} %fusion.32, f32[16,256]{1,0:T(8,128)S(1)} %get-tuple-element.76), kind=kOutput, calls=%fused_computation.41 | convolution fusion | flops 206962688 | bytes 6651904 | tf_op jit(solution)/shard_map/hqk,khd->hqd/dot_general | solution.py:62
  32.1 228.0 %while.18 = (s32[]{:T(128)}, f32[16,256]{1,0:T(8,128)S(1)}, f32[16,256]{1,0:T(8,128)S(1)}, f32[16,256,96]{1,2,0:T(8,128)}, bf16[2,256,1536]{1,2,0:T(8,128)(2,1)}...) while((s32[]{:T(128)}, f32[16,256]{1,0:T(8,128)S(1)}, ...), condition=%wide.region_8.9_spmd, body=%wide.region_5.8_spmd.sunk | while | flops 417144832 | bytes 43786468 | solution.py:116
  32.1 1.9 collective-permute-start.1
  34.0 2.9 collective-permute-start
  36.8 18.1 %collective-permute-done = s32[256]{0:T(256)S(1)} collective-permute-done((s32[256]{0:T(256)S(1)}, s32[256]{0:T(256)S(1)}, u32[]{:S(2)}, u32[]{:S(2)}) %collective-permute-start) | collective-permute-done | bytes 1056 | tf_op jit(solution)/shard_map/while/body/eval_jaxpr/ppermute | solution.py:21
  60.6 1.9 collective-permute-start.1
  62.5 2.0 collective-permute-start
  64.4 19.0 %collective-permute-done = s32[256]{0:T(256)S(1)} collective-permute-done((s32[256]{0:T(256)S(1)}, s32[256]{0:T(256)S(1)}, u32[]{:S(2)}, u32[]{:S(2)}) %collective-permute-start) | collective-permute-done | bytes 1056 | tf_op jit(solution)/shard_map/while/body/eval_jaxpr/ppermute | solution.py:21
  91.0 1.9 collective-permute-start
  92.9 19.0 %collective-permute-done = s32[256]{0:T(256)S(1)} collective-permute-done((s32[256]{0:T(256)S(1)}, s32[256]{0:T(256)S(1)}, u32[]{:S(2)}, u32[]{:S(2)}) %collective-permute-start) | collective-permute-done | bytes 1056 | tf_op jit(solution)/shard_map/while/body/eval_jaxpr/ppermute | solution.py:21
  119.5 1.9 collective-permute-start
  121.4 19.0 %collective-permute-done = s32[256]{0:T(256)S(1)} collective-permute-done((s32[256]{0:T(256)S(1)}, s32[256]{0:T(256)S(1)}, u32[]{:S(2)}, u32[]{:S(2)}) %collective-permute-start) | collective-permute-done | bytes 1056 | tf_op jit(solution)/shard_map/while/body/eval_jaxpr/ppermute | solution.py:21
  148.0 1.9 collective-permute-start
  149.9 19.0 %collective-permute-done = s32[256]{0:T(256)S(1)} collective-permute-done((s32[256]{0:T(256)S(1)}, s32[256]{0:T(256)S(1)}, u32[]{:S(2)}, u32[]{:S(2)}) %collective-permute-start) | collective-permute-done | bytes 1056 | tf_op jit(solution)/shard_map/while/body/eval_jaxpr/ppermute | solution.py:21
  176.5 1.9 collective-permute-start
  178.4 19.0 %collective-permute-done = s32[256]{0:T(256)S(1)} collective-permute-done((s32[256]{0:T(256)S(1)}, s32[256]{0:T(256)S(1)}, u32[]{:S(2)}, u32[]{:S(2)}) %collective-permute-start) | collective-permute-done | bytes 1056 | tf_op jit(solution)/shard_map/while/body/eval_jaxpr/ppermute | solution.py:21
  205.0 1.9 collective-permute-start
  206.9 19.0 %collective-permute-done = s32[256]{0:T(256)S(1)} collective-permute-done((s32[256]{0:T(256)S(1)}, s32[256]{0:T(256)S(1)}, u32[]{:S(2)}, u32[]{:S(2)}) %collective-permute-start) | collective-permute-done | bytes 1056 | tf_op jit(solution)/shard_map/while/body/eval_jaxpr/ppermute | solution.py:21
  233.4 1.9 collective-permute-start
  235.4 19.0 %collective-permute-done = s32[256]{0:T(256)S(1)} collective-permute-done((s32[256]{0:T(256)S(1)}, s32[256]{0:T(256)S(1)}, u32[]{:S(2)}, u32[]{:S(2)}) %collective-permute-start) | collective-permute-done | bytes 1056 | tf_op jit(solution)/shard_map/while/body/eval_jaxpr/ppermute | solution.py:21
  261.6 7.5 %convolution_convert_fusion = bf16[256,3072]{1,0:T(8,128)(2,1)} fusion(bf16[256,1536]{0,1:T(8,128)(2,1)S(1)} %bitcast.39, bf16[1536,3072]{1,0:T(8,128)(2,1)} %param.15), kind=kOutput, calls=%fused_computation.21 | convolution fusion | flops 2416705536 | bytes 11796480 | tf_op jit(solution)/shard_map/dot_general | solution.py:125
  271.8 48.1 %all-reduce.2.cloned.1.call-done = bf16[256,3072]{1,0:T(8,128)(2,1)} async-done(((bf16[256,3072]{1,0:T(8,128)(2,1)}), bf16[256,3072]{1,0:T(8,128)(2,1)}) %all-reduce.2.cloned.1.call-update) | async-done | bytes 1572880 | tf_op jit(solution)/shard_map/psum | solution.py:127
  321.7 4.9 %psum.15 = f32[256]{0:T(256)S(1)} all-reduce(f32[256]{0:T(256)S(1)} %get-tuple-element.66), channel_id=1, replica_groups=mesh['seq'=16,'tp'=2] {'tp'}, use_global_device_ids=true, to_apply=%region_11.12 | all-reduce | flops 256 | bytes 2048 | tf_op jit(solution)/shard_map/psum | solution.py:133
  (179 shorter events, 72.9 us)
Async XLA Ops:
  7.2 312.8 %all-reduce.2.cloned.1.call-start = ((), (), s32[]{:S(2)}) async-start(), calls=%async_computation | async-start | bytes 3145728 | tf_op jit(solution)/shard_map/psum | solution.py:127
  24.0 1.9 copy-start.1
  24.1 1.9 copy-start.2
  32.1 23.0 %collective-permute-start.1 = (bf16[2,256,1536]{1,2,0:T(8,128)(2,1)}, bf16[2,256,1536]{1,2,0:T(8,128)(2,1)S(1)}, u32[]{:S(2)}, u32[]{:S(2)}) collective-permute-start(bf16[2,256,1536]{1,2,0:T(8,128)(2,1)} %get-tuple-element.159), channel_id=1, source_target_pairs={{0,2},{2,4},{4,6},{6,8},{8,10},{10,12},{12,14},{14,16},{16,18},{18... | collective-permute-start | bytes 4718600 | tf_op jit(solution)/shard_map/while/body/eval_jaxpr/ppermute | solution.py:21
  34.0 21.0 %collective-permute-start = (s32[256]{0:T(256)S(1)}, s32[256]{0:T(256)S(1)}, u32[]{:S(2)}, u32[]{:S(2)}) collective-permute-start(s32[256]{0:T(256)S(1)} %get-tuple-element.160), channel_id=1, source_target_pairs={{0,2},{2,4},{4,6},{6,8},{8,10},{10,12},{12,14},{14,16},{16,18},{18... | collective-permute-start | bytes 3080 | tf_op jit(solution)/shard_map/while/body/eval_jaxpr/ppermute | solution.py:21
  58.9 1.7 copy-start.6
  60.6 23.0 %collective-permute-start.1 = (bf16[2,256,1536]{1,2,0:T(8,128)(2,1)}, bf16[2,256,1536]{1,2,0:T(8,128)(2,1)S(1)}, u32[]{:S(2)}, u32[]{:S(2)}) collective-permute-start(bf16[2,256,1536]{1,2,0:T(8,128)(2,1)} %get-tuple-element.159), channel_id=1, source_target_pairs={{0,2},{2,4},{4,6},{6,8},{8,10},{10,12},{12,14},{14,16},{16,18},{18... | collective-permute-start | bytes 4718600 | tf_op jit(solution)/shard_map/while/body/eval_jaxpr/ppermute | solution.py:21
  62.5 21.0 %collective-permute-start = (s32[256]{0:T(256)S(1)}, s32[256]{0:T(256)S(1)}, u32[]{:S(2)}, u32[]{:S(2)}) collective-permute-start(s32[256]{0:T(256)S(1)} %get-tuple-element.160), channel_id=1, source_target_pairs={{0,2},{2,4},{4,6},{6,8},{8,10},{10,12},{12,14},{14,16},{16,18},{18... | collective-permute-start | bytes 3080 | tf_op jit(solution)/shard_map/while/body/eval_jaxpr/ppermute | solution.py:21
  87.4 1.7 copy-start.6
  89.0 23.0 %collective-permute-start.1 = (bf16[2,256,1536]{1,2,0:T(8,128)(2,1)}, bf16[2,256,1536]{1,2,0:T(8,128)(2,1)S(1)}, u32[]{:S(2)}, u32[]{:S(2)}) collective-permute-start(bf16[2,256,1536]{1,2,0:T(8,128)(2,1)} %get-tuple-element.159), channel_id=1, source_target_pairs={{0,2},{2,4},{4,6},{6,8},{8,10},{10,12},{12,14},{14,16},{16,18},{18... | collective-permute-start | bytes 4718600 | tf_op jit(solution)/shard_map/while/body/eval_jaxpr/ppermute | solution.py:21
  91.0 21.0 %collective-permute-start = (s32[256]{0:T(256)S(1)}, s32[256]{0:T(256)S(1)}, u32[]{:S(2)}, u32[]{:S(2)}) collective-permute-start(s32[256]{0:T(256)S(1)} %get-tuple-element.160), channel_id=1, source_target_pairs={{0,2},{2,4},{4,6},{6,8},{8,10},{10,12},{12,14},{14,16},{16,18},{18... | collective-permute-start | bytes 3080 | tf_op jit(solution)/shard_map/while/body/eval_jaxpr/ppermute | solution.py:21
  117.5 23.0 %collective-permute-start.1 = (bf16[2,256,1536]{1,2,0:T(8,128)(2,1)}, bf16[2,256,1536]{1,2,0:T(8,128)(2,1)S(1)}, u32[]{:S(2)}, u32[]{:S(2)}) collective-permute-start(bf16[2,256,1536]{1,2,0:T(8,128)(2,1)} %get-tuple-element.159), channel_id=1, source_target_pairs={{0,2},{2,4},{4,6},{6,8},{8,10},{10,12},{12,14},{14,16},{16,18},{18... | collective-permute-start | bytes 4718600 | tf_op jit(solution)/shard_map/while/body/eval_jaxpr/ppermute | solution.py:21
  119.5 21.0 %collective-permute-start = (s32[256]{0:T(256)S(1)}, s32[256]{0:T(256)S(1)}, u32[]{:S(2)}, u32[]{:S(2)}) collective-permute-start(s32[256]{0:T(256)S(1)} %get-tuple-element.160), channel_id=1, source_target_pairs={{0,2},{2,4},{4,6},{6,8},{8,10},{10,12},{12,14},{14,16},{16,18},{18... | collective-permute-start | bytes 3080 | tf_op jit(solution)/shard_map/while/body/eval_jaxpr/ppermute | solution.py:21
  146.0 23.0 %collective-permute-start.1 = (bf16[2,256,1536]{1,2,0:T(8,128)(2,1)}, bf16[2,256,1536]{1,2,0:T(8,128)(2,1)S(1)}, u32[]{:S(2)}, u32[]{:S(2)}) collective-permute-start(bf16[2,256,1536]{1,2,0:T(8,128)(2,1)} %get-tuple-element.159), channel_id=1, source_target_pairs={{0,2},{2,4},{4,6},{6,8},{8,10},{10,12},{12,14},{14,16},{16,18},{18... | collective-permute-start | bytes 4718600 | tf_op jit(solution)/shard_map/while/body/eval_jaxpr/ppermute | solution.py:21
  148.0 21.0 %collective-permute-start = (s32[256]{0:T(256)S(1)}, s32[256]{0:T(256)S(1)}, u32[]{:S(2)}, u32[]{:S(2)}) collective-permute-start(s32[256]{0:T(256)S(1)} %get-tuple-element.160), channel_id=1, source_target_pairs={{0,2},{2,4},{4,6},{6,8},{8,10},{10,12},{12,14},{14,16},{16,18},{18... | collective-permute-start | bytes 3080 | tf_op jit(solution)/shard_map/while/body/eval_jaxpr/ppermute | solution.py:21
  174.5 23.0 %collective-permute-start.1 = (bf16[2,256,1536]{1,2,0:T(8,128)(2,1)}, bf16[2,256,1536]{1,2,0:T(8,128)(2,1)S(1)}, u32[]{:S(2)}, u32[]{:S(2)}) collective-permute-start(bf16[2,256,1536]{1,2,0:T(8,128)(2,1)} %get-tuple-element.159), channel_id=1, source_target_pairs={{0,2},{2,4},{4,6},{6,8},{8,10},{10,12},{12,14},{14,16},{16,18},{18... | collective-permute-start | bytes 4718600 | tf_op jit(solution)/shard_map/while/body/eval_jaxpr/ppermute | solution.py:21
  176.5 21.0 %collective-permute-start = (s32[256]{0:T(256)S(1)}, s32[256]{0:T(256)S(1)}, u32[]{:S(2)}, u32[]{:S(2)}) collective-permute-start(s32[256]{0:T(256)S(1)} %get-tuple-element.160), channel_id=1, source_target_pairs={{0,2},{2,4},{4,6},{6,8},{8,10},{10,12},{12,14},{14,16},{16,18},{18... | collective-permute-start | bytes 3080 | tf_op jit(solution)/shard_map/while/body/eval_jaxpr/ppermute | solution.py:21
  203.0 23.0 %collective-permute-start.1 = (bf16[2,256,1536]{1,2,0:T(8,128)(2,1)}, bf16[2,256,1536]{1,2,0:T(8,128)(2,1)S(1)}, u32[]{:S(2)}, u32[]{:S(2)}) collective-permute-start(bf16[2,256,1536]{1,2,0:T(8,128)(2,1)} %get-tuple-element.159), channel_id=1, source_target_pairs={{0,2},{2,4},{4,6},{6,8},{8,10},{10,12},{12,14},{14,16},{16,18},{18... | collective-permute-start | bytes 4718600 | tf_op jit(solution)/shard_map/while/body/eval_jaxpr/ppermute | solution.py:21
  205.0 21.0 %collective-permute-start = (s32[256]{0:T(256)S(1)}, s32[256]{0:T(256)S(1)}, u32[]{:S(2)}, u32[]{:S(2)}) collective-permute-start(s32[256]{0:T(256)S(1)} %get-tuple-element.160), channel_id=1, source_target_pairs={{0,2},{2,4},{4,6},{6,8},{8,10},{10,12},{12,14},{14,16},{16,18},{18... | collective-permute-start | bytes 3080 | tf_op jit(solution)/shard_map/while/body/eval_jaxpr/ppermute | solution.py:21
  229.9 1.7 copy-start.6
  231.5 23.0 %collective-permute-start.1 = (bf16[2,256,1536]{1,2,0:T(8,128)(2,1)}, bf16[2,256,1536]{1,2,0:T(8,128)(2,1)S(1)}, u32[]{:S(2)}, u32[]{:S(2)}) collective-permute-start(bf16[2,256,1536]{1,2,0:T(8,128)(2,1)} %get-tuple-element.159), channel_id=1, source_target_pairs={{0,2},{2,4},{4,6},{6,8},{8,10},{10,12},{12,14},{14,16},{16,18},{18... | collective-permute-start | bytes 4718600 | tf_op jit(solution)/shard_map/while/body/eval_jaxpr/ppermute | solution.py:21
  233.4 21.0 %collective-permute-start = (s32[256]{0:T(256)S(1)}, s32[256]{0:T(256)S(1)}, u32[]{:S(2)}, u32[]{:S(2)}) collective-permute-start(s32[256]{0:T(256)S(1)} %get-tuple-element.160), channel_id=1, source_target_pairs={{0,2},{2,4},{4,6},{6,8},{8,10},{10,12},{12,14},{14,16},{16,18},{18... | collective-permute-start | bytes 3080 | tf_op jit(solution)/shard_map/while/body/eval_jaxpr/ppermute | solution.py:21
  271.8 56.0 %copy-start = (bf16[2,2,128,1536]{3,2,1,0:T(8,128)(2,1)}, bf16[2,2,128,1536]{3,2,1,0:T(8,128)(2,1)S(1)}, u32[]{:S(2)}) copy-start(bf16[2,2,128,1536]{3,2,1,0:T(8,128)(2,1)S(1)} %scatter_fusion) | copy-start | bytes 4718596
  321.7 6.1 %copy-start.4 = (bf16[256,1536]{1,0:T(8,128)(2,1)}, bf16[256,1536]{1,0:T(8,128)(2,1)S(1)}, u32[]{:S(2)}) copy-start(bf16[256,1536]{1,0:T(8,128)(2,1)S(1)} %get-tuple-element.67) | copy-start | bytes 2359300
  (18 other events, 24.2 us)
Sparse Core Ops, SparseCore 0:
  269.2 50.6 all-reduce.1
where the time goes:
time: 337 us; the launch traced here: 335 us
  waiting for transfers between devices  199 us (59%)
  starting transfers between devices  31.7 us (9%)
  matrix products  31.1 us (9%)
  local copies, waits for them, and re-layouts  23.5 us (7%)
  other arithmetic  18.8 us (6%)
  blocking collectives  15 us (4%)
  between operations  14.3 us (4%)
    ppermute x16, waiting for transfers between devices, passed_along(): return lax.ppermute(block, axis, route)  151 us
    psum x1, waiting for transfers between devices, per_device(): lax.psum(partial_value.astype(jnp.bfloat16), 'tp').astype(jnp.float32)  48.1 us
    ppermute x16, starting transfers between devices, passed_along(): return lax.ppermute(block, axis, route)  31.6 us
    while x56, local copies, waits for them, and re-layouts  16 us
    dot_general x9, matrix products, attend(): jnp.einsum('hqk,khd->hqd', unnormed.astype(jnp.bfloat16), val_heads, pref...  15.5 us
    pmin x1, blocking collectives, per_device(): first_tok = lax.pmin(local_first, 'seq')  10.1 us
    reduce_sum x9, other arithmetic, attend(): row_total = row_total * rescale + jnp.sum(unnormed, axis=-1)  9.19 us
    dot_general x9, matrix products, attend(): jnp.einsum('qhd,khd->hqk', query_heads, key_heads, preferred_element_type...  8.1 us
  transfers between devices with their start and end apart: 17, of which 9 were waited for; matrix products, arithmetic and copies ran while one was open for 1% of the time, Pallas kernels for 0%

commit v1 on v0

v1 whole, which is shorter than its diff:
```python
import functools
import math

import jax
import jax.numpy as jnp
from jax import lax
from jax.experimental import pallas as pl
from jax.experimental.pallas import tpu as pltpu
from jax.sharding import PartitionSpec as P

D = 3072
HEAD_DIM = 96
HALF = HEAD_DIM // 2
PAGE = 128
LEVEL = 4
CHUNKS = 4
COLS = 384

far_index = 1073741824
masked_score = -1e30
norm_epsilon = 1e-05
MESH = pl.DeviceIdType.MESH


def rotate(values_in, position, head_count, head_dim):
    count_rows = values_in.shape[0]
    half_dim = head_dim // 2
    frequency = jnp.exp(
        jnp.arange(half_dim, dtype=jnp.float32) * (-2.0 * math.log(10000.0) / head_dim)
    )
    angles = position.astype(jnp.float32)[:, None] * frequency[None, :]
    cosine = jnp.cos(angles)[:, None, :]
    sine_part = jnp.sin(angles)[:, None, :]
    as_float = values_in.astype(jnp.float32).reshape(count_rows, head_count, head_dim)
    lower_half = as_float[..., :half_dim]
    upper_half = as_float[..., half_dim:]
    rotated = jnp.concatenate(
        [
            lower_half * cosine - upper_half * sine_part,
            upper_half * cosine + lower_half * sine_part,
        ],
        axis=-1,
    )
    return rotated.reshape(count_rows, head_count * head_dim).astype(jnp.bfloat16)


def kernel(
    seq,
    tp,
    q_ref,
    k_ref,
    v_ref,
    hid_ref,
    gain_ref,
    cos_ref,
    sin_ref,
    kaug_ref,
    qaug_ref,
    bias_ref,
    w_hbm,
    out_ref,
    norm_ref,
    kv,
    qx,
    flip,
    attn,
    m_s,
    l_s,
    acc,
    w_s,
    own_p,
    sbuf,
    rbuf,
    ssq_s,
    ssq_r,
    w_sem,
    z_send,
    y_send,
    c_send,
    d_send,
    recv,
    p_send,
    p_recv,
    s_send,
    s_recv,
):
    tok, feat = q_ref.shape
    heads = feat // HEAD_DIM
    hc = heads // CHUNKS
    fc = hc * HEAD_DIM
    aug = kaug_ref.shape[0]
    reach = seq // (2 * LEVEL)
    nt = feat // COLS
    me = lax.axis_index("seq")
    me_tp = lax.axis_index("tp")
    z = me // LEVEL
    m = me % LEVEL
    my = m // 2
    mc = m % 2
    core_mem = my * 2 + (1 - mc)
    y_mem = (1 - my) * 2 + mc
    diag_mem = (1 - my) * 2 + (1 - mc)
    core_dev = z * LEVEL + core_mem
    y_dev = z * LEVEL + y_mem
    last_z = seq // LEVEL - 1

    w_copy = pltpu.make_async_copy(w_hbm, w_s, w_sem)
    w_copy.start()

    barrier = pltpu.get_barrier_semaphore()
    for dev in (core_dev, y_dev):
        pl.semaphore_signal(barrier, inc=1, device_id=(dev, me_tp), device_id_type=MESH)
    for j in range(1, tp):
        pl.semaphore_signal(
            barrier, inc=1, device_id=(me, (me_tp + j) % tp), device_id_type=MESH
        )

    @pl.when(z > 0)
    def _():
        pl.semaphore_signal(barrier, inc=1, device_id=(me - LEVEL, me_tp), device_id_type=MESH)

    @pl.when(z < last_z)
    def _():
        pl.semaphore_signal(barrier, inc=1, device_id=(me + LEVEL, me_tp), device_id_type=MESH)

    flip[...] = v_ref[...].T
    for ch in range(CHUNKS):
        kv[m, ch, pl.ds(fc, fc), :] = flip[pl.ds(ch * fc, fc), :]
        kv[m, ch, pl.ds(2 * fc, aug), :] = kaug_ref[...]
    flip[...] = k_ref[...].T
    cosine = cos_ref[...]
    sine = sin_ref[...]

    peers = 1 + tp + (z > 0).astype(jnp.int32) + (z < last_z).astype(jnp.int32)
    pl.semaphore_wait(barrier, peers)

    def move(src_slot, dst_slot, ch, sem, dev):
        return pltpu.make_async_remote_copy(
            src_ref=kv.at[src_slot, ch],
            dst_ref=kv.at[dst_slot, ch],
            send_sem=sem,
            recv_sem=recv.at[dst_slot, ch],
            device_id=(dev, me_tp),
            device_id_type=MESH,
        )

    def z_copy(lev, ch):
        return move(lev * LEVEL + m, (lev + 1) * LEVEL + m, ch, z_send.at[lev, ch], me + LEVEL)

    def y_copy(lev, ch):
        slot = lev * LEVEL + m
        return move(slot, slot, ch, y_send.at[lev, ch], y_dev)

    def c_copy(lev, ch):
        slot = lev * LEVEL + m
        return move(slot, slot, ch, c_send.at[lev, ch], core_dev)

    def d_copy(lev, ch):
        slot = lev * LEVEL + y_mem
        return move(slot, slot, ch, d_send.at[lev, ch], core_dev)

    def arrived(slot, ch):
        pltpu.make_async_remote_copy(
            src_ref=kv.at[slot, ch],
            dst_ref=kv.at[slot, ch],
            send_sem=z_send.at[0, 0],
            recv_sem=recv.at[slot, ch],
            device_id=(core_dev, me_tp),
            device_id_type=MESH,
        ).wait_recv()

    def z_on(lev):
        return (z - lev >= 0) & (z < last_z) & (lev < reach)

    def band(lev, src, dst):
        return (z - lev >= 0) & ((lev > 0) | (src <= dst)) & ((lev < reach) | (src >= dst))

    def y_on(lev):
        return band(lev, my, 1 - my)

    def b_on(lev):
        return band(lev, 1 - my, my)

    def c_on(lev):
        return band(lev, mc, 1 - mc)

    def cr_on(lev):
        return band(lev, 1 - mc, mc)

    def send_column(lev, ch):
        @pl.when(z_on(lev))
        def _():
            z_copy(lev, ch).start()

        @pl.when(y_on(lev))
        def _():
            y_copy(lev, ch).start()

        @pl.when(c_on(lev))
        def _():
            c_copy(lev, ch).start()

    def turned(x, scale):
        low = x[:HALF].astype(jnp.float32)
        high = x[HALF:].astype(jnp.float32)
        return (
            ((low * cosine - high * sine) * scale).astype(jnp.bfloat16),
            ((high * cosine + low * sine) * scale).astype(jnp.bfloat16),
        )

    for ch in range(CHUNKS):
        for hh in range(hc):
            first, second = turned(flip[pl.ds((ch * hc + hh) * HEAD_DIM, HEAD_DIM), :], 1.0)
            kv[m, ch, pl.ds(hh * HEAD_DIM, HALF), :] = first
            kv[m, ch, pl.ds(hh * HEAD_DIM + HALF, HALF), :] = second
        send_column(0, ch)

    flip[...] = q_ref[...].T
    for h in range(heads):
        first, second = turned(
            flip[pl.ds(h * HEAD_DIM, HEAD_DIM), :], math.log2(math.e) / math.sqrt(HEAD_DIM)
        )
        qx[h, pl.ds(0, HALF), :] = first
        qx[h, pl.ds(HALF, HALF), :] = second
        qx[h, pl.ds(HEAD_DIM, aug), :] = qaug_ref[...]

    cross = (((0,), (0,)), ((), ()))

    def own_chunk(ch, carry):
        for hh in range(hc):
            h = ch * hc + hh
            keys = kv[m, ch, pl.ds(hh * HEAD_DIM, HEAD_DIM), :]
            s = lax.dot_general(
                keys, qx[h, pl.ds(0, HEAD_DIM), :], cross, preferred_element_type=jnp.float32
            )
            s = s + bias_ref[...]
            peak = jnp.max(s, axis=0, keepdims=True)
            p = jnp.exp2(s - peak)
            m_s[h] = peak
            l_s[h] = jnp.sum(p, axis=0, keepdims=True)
            acc[h] = jnp.dot(
                kv[m, ch, pl.ds(fc + hh * HEAD_DIM, HEAD_DIM), :],
                p.astype(jnp.bfloat16),
                preferred_element_type=jnp.float32,
            )
        return carry

    lax.fori_loop(0, CHUNKS, own_chunk, 0)

    def tile(slot, ch):
        tags = kv[slot, ch, pl.ds(2 * fc, aug), :]
        for hh in range(hc):
            h = ch * hc + hh
            keys = jnp.concatenate([kv[slot, ch, pl.ds(hh * HEAD_DIM, HEAD_DIM), :], tags], axis=0)
            s = lax.dot_general(keys, qx[h], cross, preferred_element_type=jnp.float32)
            old = m_s[h]
            peak = jnp.maximum(old, jnp.max(s, axis=0, keepdims=True))
            rescale = jnp.exp2(old - peak)
            p = jnp.exp2(s - peak)
            m_s[h] = peak
            l_s[h] = l_s[h] * rescale + jnp.sum(p, axis=0, keepdims=True)
            acc[h] = acc[h] * rescale + jnp.dot(
                kv[slot, ch, pl.ds(fc + hh * HEAD_DIM, HEAD_DIM), :],
                p.astype(jnp.bfloat16),
                preferred_element_type=jnp.float32,
            )

    def step(g, carry):
        lev = g // CHUNKS
        ch = g % CHUNKS
        nxt = lev + 1
        a_on = (nxt <= reach) & (z - nxt >= 0)
        b_in = b_on(lev)
        c_in = cr_on(lev)

        @pl.when(a_on)
        def _():
            arrived(nxt * LEVEL + m, ch)
            send_column(nxt, ch)

        @pl.when(b_in)
        def _():
            arrived(lev * LEVEL + y_mem, ch)
            d_copy(lev, ch).start()

        @pl.when(a_on)
        def _():
            tile(nxt * LEVEL + m, ch)

        @pl.when(b_in)
        def _():
            tile(lev * LEVEL + y_mem, ch)

        @pl.when(c_in)
        def _():
            arrived(lev * LEVEL + core_mem, ch)
            tile(lev * LEVEL + core_mem, ch)

        @pl.when(b_in)
        def _():
            arrived(lev * LEVEL + diag_mem, ch)
            tile(lev * LEVEL + diag_mem, ch)

        return carry

    lax.fori_loop(0, (reach + 1) * CHUNKS, step, 0)

    for h in range(heads):
        flip[pl.ds(h * HEAD_DIM, HEAD_DIM), :] = (acc[h] / l_s[h]).astype(jnp.bfloat16)
    w_copy.wait()
    attn[...] = flip[...].T

    def p_copy(j, t):
        return pltpu.make_async_remote_copy(
            src_ref=sbuf.at[j - 1, t],
            dst_ref=rbuf.at[j - 1, t],
            send_sem=p_send.at[j - 1, t],
            recv_sem=p_recv.at[j - 1, t],
            device_id=(me, (me_tp + j) % tp),
            device_id_type=MESH,
        )

    def product(to, t):
        start = pl.multiple_of(to * feat + t * COLS, COLS)
        return jnp.dot(attn[...], w_s[:, pl.ds(start, COLS)], preferred_element_type=jnp.float32)

    for j in range(1, tp):

        def give(t, carry):
            sbuf[j - 1, t] = product((me_tp + j) % tp, t).astype(jnp.bfloat16)
            p_copy(j, t).start()
            return carry

        lax.fori_loop(0, nt, give, 0)

    def keep(t, carry):
        own_p[t] = product(me_tp, t)
        return carry

    lax.fori_loop(0, nt, keep, 0)

    square = jnp.zeros((tok, 1), jnp.float32)
    for t in range(nt):
        total = own_p[t]
        for j in range(1, tp):
            p_copy(j, t).wait_recv()
            total = total + rbuf[j - 1, t].astype(jnp.float32)
        cols = pl.ds(t * COLS, COLS)
        fresh = (hid_ref[:, cols].astype(jnp.float32) + total).astype(jnp.bfloat16)
        out_ref[:, cols] = fresh
        wide = fresh.astype(jnp.float32)
        square = square + jnp.sum(wide * wide, axis=1, keepdims=True)

    ssq_s[...] = jnp.broadcast_to(square, (tok, 128)).T[:8]

    def s_copy(j):
        return pltpu.make_async_remote_copy(
            src_ref=ssq_s,
            dst_ref=ssq_r.at[j - 1],
            send_sem=s_send.at[j - 1],
            recv_sem=s_recv.at[j - 1],
            device_id=(me, (me_tp + j) % tp),
            device_id_type=MESH,
        )

    for j in range(1, tp):
        s_copy(j).start()

    def drain(g, carry):
        lev = g // CHUNKS
        ch = g % CHUNKS

        @pl.when(z_on(lev))
        def _():
            z_copy(lev, ch).wait_send()

        @pl.when(y_on(lev))
        def _():
            y_copy(lev, ch).wait_send()

        @pl.when(c_on(lev))
        def _():
            c_copy(lev, ch).wait_send()

        @pl.when(b_on(lev))
        def _():
            d_copy(lev, ch).wait_send()

        return carry

    lax.fori_loop(0, (reach + 1) * CHUNKS, drain, 0)
    for j in range(1, tp):
        for t in range(nt):
            p_copy(j, t).wait_send()

    sums = ssq_s[...]
    for j in range(1, tp):
        s_copy(j).wait()
        sums = sums + ssq_r[j - 1]
    inverse = lax.rsqrt(sums / D + norm_epsilon)
    inverse = jnp.concatenate([inverse] * 16, axis=0).T[:, :1]
    for t in range(nt):
        cols = pl.ds(t * COLS, COLS)
        norm_ref[:, cols] = (
            out_ref[:, cols].astype(jnp.float32)
            * inverse
            * gain_ref[:, cols].astype(jnp.float32)
        ).astype(jnp.bfloat16)


def per_device(
    query_proj,
    key_proj,
    value_proj,
    hidden,
    out_weight,
    norm_gain,
    segment_ids,
    pad_mask,
    page_table,
):
    tok_count = query_proj.shape[0]
    feat_count = query_proj.shape[1]
    head_count = feat_count // HEAD_DIM
    seq = lax.axis_size("seq")
    tp = lax.axis_size("tp")
    seg_count = seq // 2
    reach = seq // (2 * LEVEL)
    device_row = lax.axis_index("seq")
    tok_index = device_row * tok_count + jnp.arange(tok_count, dtype=jnp.int32)
    member = segment_ids[:, None] == jnp.arange(seg_count, dtype=jnp.int32)[None, :]
    local_first = jnp.min(jnp.where(member, tok_index[:, None], far_index), axis=0)
    first_tok = lax.pmin(local_first, "seq")

    frequency = jnp.exp(
        jnp.arange(HALF, dtype=jnp.float32) * (-2.0 * math.log(10000.0) / HEAD_DIM)
    )
    angles = frequency[:, None] * tok_index.astype(jnp.float32)[None, :]
    cosine, sine = jnp.cos(angles), jnp.sin(angles)
    aug = max(16, seg_count)
    tags = jnp.where(pad_mask == 1, segment_ids, -1)
    slots = jnp.arange(aug, dtype=jnp.int32)[:, None]
    kaug = (slots != tags[None, :]).astype(jnp.bfloat16)
    qaug = jnp.where(slots == segment_ids[None, :], masked_score, 0.0).astype(jnp.bfloat16)
    offsets = jnp.arange(tok_count, dtype=jnp.int32)
    own_visible = (tags[:, None] == segment_ids[None, :]) & (
        offsets[:, None] <= offsets[None, :]
    ) | (offsets[:, None] == offsets[None, :])
    bias = jnp.where(own_visible, 0.0, masked_score).astype(jnp.float32)

    hc = head_count // CHUNKS
    fc = hc * HEAD_DIM
    nt = feat_count // COLS
    n_slots = (reach + 1) * LEVEL
    vm = pl.BlockSpec(memory_space=pltpu.VMEM)
    dma = pltpu.SemaphoreType.DMA
    flops = 4 * head_count * 9 * tok_count * tok_count * HEAD_DIM
    hidden_out, normed = pl.pallas_call(
        functools.partial(kernel, seq, tp),
        out_shape=[jax.ShapeDtypeStruct((tok_count, feat_count), jnp.bfloat16)] * 2,
        in_specs=[vm] * 10 + [pl.BlockSpec(memory_space=pl.ANY)],
        out_specs=[vm, vm],
        scratch_shapes=[
            pltpu.VMEM((n_slots, CHUNKS, 2 * fc + aug, tok_count), jnp.bfloat16),
            pltpu.VMEM((head_count, HEAD_DIM + aug, tok_count), jnp.bfloat16),
            pltpu.VMEM((feat_count, tok_count), jnp.bfloat16),
            pltpu.VMEM((tok_count, feat_count), jnp.bfloat16),
            pltpu.VMEM((head_count, 1, tok_count), jnp.float32),
            pltpu.VMEM((head_count, 1, tok_count), jnp.float32),
            pltpu.VMEM((head_count, HEAD_DIM, tok_count), jnp.float32),
            pltpu.VMEM(out_weight.shape, jnp.bfloat16),
            pltpu.VMEM((nt, tok_count, COLS), jnp.float32),
            pltpu.VMEM((tp - 1, nt, tok_count, COLS), jnp.bfloat16),
            pltpu.VMEM((tp - 1, nt, tok_count, COLS), jnp.bfloat16),
            pltpu.VMEM((8, tok_count), jnp.float32),
            pltpu.VMEM((tp - 1, 8, tok_count), jnp.float32),
            dma,
            dma((reach + 1, CHUNKS)),
            dma((reach + 1, CHUNKS)),
            dma((reach + 1, CHUNKS)),
            dma((reach + 1, CHUNKS)),
            dma((n_slots, CHUNKS)),
            dma((tp - 1, nt)),
            dma((tp - 1, nt)),
            dma((tp - 1,)),
            dma((tp - 1,)),
        ],
        compiler_params=pltpu.CompilerParams(
            collective_id=0, has_side_effects=True, vmem_limit_bytes=56 * 1024 * 1024
        ),
        cost_estimate=pl.CostEstimate(
            flops=flops, bytes_accessed=16 * 1024 * 1024, transcendentals=0
        ),
    )(
        query_proj,
        key_proj,
        value_proj,
        hidden,
        norm_gain[None, :],
        cosine,
        sine,
        kaug,
        qaug,
        bias,
        out_weight,
    )

    position = tok_index - jnp.sum(jnp.where(member, first_tok[None, :], 0), axis=1)
    k_rot = rotate(key_proj, position, head_count, HEAD_DIM)
    pad_scale = pad_mask.astype(jnp.bfloat16)[:, None]
    page_count = tok_count // PAGE
    stacked = jnp.stack([k_rot * pad_scale, value_proj * pad_scale])
    stacked = stacked.reshape(2, page_count, PAGE, feat_count).transpose(1, 0, 2, 3)
    kv_pages = jnp.zeros_like(stacked).at[page_table].set(stacked)
    return (hidden_out, normed, kv_pages)


def solution(mesh):
    placed = (
        P("seq", "tp"),
        P("seq", "tp"),
        P("seq", "tp"),
        P("seq", "tp"),
        P("tp", None),
        P("tp"),
        P("seq"),
        P("seq"),
        P("seq"),
    )
    return jax.shard_map(
        per_device,
        mesh=mesh,
        in_specs=placed,
        out_specs=(P("seq", "tp"), P("seq", "tp"), P("seq", None, None, "tp")),
        check_vma=False,
    )
```

time: 337 us -> 148 us (0.44)
  waiting for transfers between devices: 199 us -> 0 us
  Pallas kernels: 0 us -> 118 us
  starting transfers between devices: 31.7 us -> 0 us
  matrix products: 31.1 us -> 0 us
  between operations: 14.3 us -> 0.83 us
  local copies, waits for them, and re-layouts: 23.5 us -> 10.1 us
  other arithmetic: 18.8 us -> 9.14 us
  blocking collectives: 15 us -> 10.1 us
    ppermute x16 -> x0, waiting for transfers between devices: 151 us -> none  [passed_along(): return lax.ppermute(block, axis, route)]
    pallas_call x0 -> x1, Pallas kernels: none -> 118 us  [per_device(): pl.pallas_call(functools.partial(kernel, seq, tp), out_shape=[jax.ShapeDt...]
    psum x1 -> x0, waiting for transfers between devices: 48.1 us -> none  [per_device(): lax.psum(partial_value.astype(jnp.bfloat16), 'tp').astype(jnp.float32)]
    ppermute x16 -> x0, starting transfers between devices: 31.6 us -> none  [passed_along(): return lax.ppermute(block, axis, route)]
    dot_general x19 -> x0, matrix products: 31.1 us -> none  [the longest x9 15.5 us: attend(): jnp.einsum('hqk,khd->hqd', unnormed.astype(jnp.bfloat16), val_heads, pref...]
    while x56 -> x0, local copies, waits for them, and re-layouts: 16 us -> none
    reduce_sum x10 -> x0, other arithmetic: 10.9 us -> none  [the longest x9 9.19 us: attend(): row_total = row_total * rescale + jnp.sum(unnormed, axis=-1)]
    psum x1 -> x0, blocking collectives: 4.94 us -> none  [per_device(): square_total = lax.psum(jnp.sum(stream_wide * stream_wide, axis=1), 'tp')]
  transfers between devices with their start and end apart: 17 -> 0, of which waited for: 9 -> 0; matrix products, arithmetic and copies ran while one was open for 1% -> 0% of each run, Pallas kernels for 0% -> 0%
where the time goes in v1:
time: 148 us
  Pallas kernels  118 us (80%)
  blocking collectives  10.1 us (7%)
  local copies, waits for them, and re-layouts  10.1 us (7%)
  other arithmetic  9.14 us (6%)
    pallas_call x1, Pallas kernels, per_device(): pl.pallas_call(functools.partial(kernel, seq, tp), out_shape=[jax.ShapeDt...  118 us
    pmin x1, blocking collectives, per_device(): first_tok = lax.pmin(local_first, 'seq')  10.1 us
    unnamed x18, local copies, waits for them, and re-layouts  5.33 us
    transpose x1, other arithmetic, per_device(): stacked.reshape(2, page_count, PAGE, feat_count).transpose(1, 0, 2, 3)  3.48 us

profile of v1, /device:TPU:16, one launch (start us, length us, event | category | flops | bytes accessed | tf_op | source)
XLA Modules:
  0.0 147.8 jit_solution(13085151847748903756)
XLA Ops:
  0.6 0.8 select_reduce_fusion.1
  1.4 10.1 %pmin.7 = s32[8]{0:T(128)S(1)} all-reduce(s32[8]{0:T(128)S(1)} %select_reduce_fusion.1), channel_id=1, replica_groups=mesh['seq'=16,'tp'=2] {'seq'}, use_global_device_ids=true, to_apply=%region_1.2 | all-reduce | flops 8 | bytes 64 | tf_op jit(solution)/shard_map/pmin | solution.py:433
  11.5 0.8 select_reduce_fusion
  12.3 0.3 multiply_cosine_fusion
  12.5 1.4 copy.16
  14.0 0.2 convert.9
  14.1 0.2 subtract_convert_fusion
  14.5 0.2 convert_element_type.40
  14.7 0.4 copy-done.3
  15.1 0.5 copy-done.1
  15.6 0.1 broadcast_multiply_fusion
  15.7 1.8 %copy.19 = bf16[1,2,128,1536]{2,1,3,0:T(2,128)(2,1)} copy(bf16[1,2,128,1536]{3,2,1,0:T(8,128)(2,1)S(1)} %bitcast.12) | data formatting | bytes 1572864 | tf_op jit(solution)/shard_map/stack | solution.py:512
  17.5 3.5 %maximum_bitcast_fusion = bf16[2,2,128,1536]{2,0,3,1:T(2,128)(2,1)S(1)} fusion(bf16[1,2,128,1536]{2,1,3,0:T(2,128)(2,1)} %copy.19, bf16[1,2,128,1536]{2,1,3,0:T(2,128)(2,1)S(1)} %bitcast.13), kind=kLoop, calls=%fused_computation.1 | loop fusion | flops 786432 | bytes 3145728 | tf_op jit(solution)/shard_map/transpose | solution.py:513
  21.0 1.2 copy.18
  22.3 0.1 broadcast_in_dim.79
  22.4 0.9 scatter_fusion
  23.3 1.2 multiply_sine_fusion.1
  24.5 0.8 fusion.2.bias_ref
  25.3 0.6 fusion.3.kaug_ref
  25.9 0.6 select_convert_fusion.qaug_ref
  26.5 0.6 broadcast_in_dim.73.gain_ref
  27.1 117.7 %shard_map.112 = (bf16[256,1536]{1,0:T(8,128)(2,1)}, bf16[256,1536]{1,0:T(8,128)(2,1)}) custom-call(bf16[256,1536]{1,0:T(8,128)(2,1)} %q_ref.1, bf16[256,1536]{1,0:T(8,128)(2,1)} %k_ref.1, bf16[256,1536]{1,0:T(8,128)(2,1)} %v_ref.1, bf16[256,1536]{1,0:T(8,128)(2,1)} %hid_ref.1, bf16[1,1536]{1,0:T(2,128)(2,1)} %broadcast_in_dim.73.gain_ref, ...), custom_call_target="tpu_custom_call" | custom-call | flops 3623878656 | bytes 16777216 | tf_op jit(solution)/shard_map/pallas_call | solution.py:458
  144.8 2.1 %copy.23 = bf16[256,1536]{1,0:T(8,128)(2,1)} copy(bf16[256,1536]{1,0:T(8,128)(2,1)} %get-tuple-element.18) | data formatting | bytes 1572864
  147.0 0.9 copy.24
  (21 shorter events, 0.2 us)
Async XLA Ops:
  14.3 0.7 copy-start.3
  14.4 0.7 copy-start.5
  14.5 1.1 copy-start.1
  21.0 1.2 copy-start.6
  22.4 4.1 %copy-start.4 = (bf16[1536]{0:T(1024)(128)(2,1)S(1)}, bf16[1536]{0:T(1024)(128)(2,1)}, u32[]{:S(2)}) copy-start(bf16[1536]{0:T(1024)(128)(2,1)} %param.14) | copy-start | bytes 9220
  23.3 121.5 %copy-start = (bf16[2,2,128,1536]{3,2,1,0:T(8,128)(2,1)}, bf16[2,2,128,1536]{3,2,1,0:T(8,128)(2,1)S(1)}, u32[]{:S(2)}) copy-start(bf16[2,2,128,1536]{3,2,1,0:T(8,128)(2,1)S(1)} %scatter_fusion) | copy-start | bytes 4718596
  144.8 2.1 %copy-start.2 = (bf16[256,1536]{1,0:T(8,128)(2,1)S(1)}, bf16[256,1536]{1,0:T(8,128)(2,1)}, u32[]{:S(2)}) copy-start(bf16[256,1536]{1,0:T(8,128)(2,1)} %get-tuple-element.19) | copy-start | bytes 2359300

commit v2 on v1

--- a/solution.py
+++ b/solution.py
@@ -13,35 +13,13 @@
 HALF = HEAD_DIM // 2
 PAGE = 128
 LEVEL = 4
-CHUNKS = 4
+CHUNK_MOST = 8
 COLS = 384
 
 far_index = 1073741824
 masked_score = -1e30
 norm_epsilon = 1e-05
 MESH = pl.DeviceIdType.MESH
-
-
-def rotate(values_in, position, head_count, head_dim):
-    count_rows = values_in.shape[0]
-    half_dim = head_dim // 2
-    frequency = jnp.exp(
-        jnp.arange(half_dim, dtype=jnp.float32) * (-2.0 * math.log(10000.0) / head_dim)
-    )
-    angles = position.astype(jnp.float32)[:, None] * frequency[None, :]
-    cosine = jnp.cos(angles)[:, None, :]
-    sine_part = jnp.sin(angles)[:, None, :]
-    as_float = values_in.astype(jnp.float32).reshape(count_rows, head_count, head_dim)
-    lower_half = as_float[..., :half_dim]
-    upper_half = as_float[..., half_dim:]
-    rotated = jnp.concatenate(
-        [
-            lower_half * cosine - upper_half * sine_part,
-            upper_half * cosine + lower_half * sine_part,
-        ],
-        axis=-1,
-    )
-    return rotated.reshape(count_rows, head_count * head_dim).astype(jnp.bfloat16)
 
 
 def kernel(
@@ -54,15 +32,21 @@
     gain_ref,
     cos_ref,
     sin_ref,
-    kaug_ref,
+    tags_ref,
     qaug_ref,
     bias_ref,
+    place_ref,
+    pad_ref,
+    table_ref,
     w_hbm,
     out_ref,
     norm_ref,
+    page_ref,
     kv,
     qx,
     flip,
+    flip_k,
+    tg,
     attn,
     m_s,
     l_s,
@@ -83,12 +67,15 @@
     p_recv,
     s_send,
     s_recv,
+    t_send,
+    t_recv,
 ):
     tok, feat = q_ref.shape
     heads = feat // HEAD_DIM
+    CHUNKS = min(CHUNK_MOST, heads)
     hc = heads // CHUNKS
     fc = hc * HEAD_DIM
-    aug = kaug_ref.shape[0]
+    aug = qaug_ref.shape[0]
     reach = seq // (2 * LEVEL)
     nt = feat // COLS
     me = lax.axis_index("seq")
@@ -103,36 +90,50 @@
     core_dev = z * LEVEL + core_mem
     y_dev = z * LEVEL + y_mem
     last_z = seq // LEVEL - 1
+    span = reach * LEVEL
 
     w_copy = pltpu.make_async_copy(w_hbm, w_s, w_sem)
     w_copy.start()
 
     barrier = pltpu.get_barrier_semaphore()
-    for dev in (core_dev, y_dev):
-        pl.semaphore_signal(barrier, inc=1, device_id=(dev, me_tp), device_id_type=MESH)
     for j in range(1, tp):
         pl.semaphore_signal(
             barrier, inc=1, device_id=(me, (me_tp + j) % tp), device_id_type=MESH
         )
-
-    @pl.when(z > 0)
-    def _():
-        pl.semaphore_signal(barrier, inc=1, device_id=(me - LEVEL, me_tp), device_id_type=MESH)
-
-    @pl.when(z < last_z)
-    def _():
-        pl.semaphore_signal(barrier, inc=1, device_id=(me + LEVEL, me_tp), device_id_type=MESH)
+    for d in range(1, span + 1):
+
+        @pl.when(me >= d)
+        def _():
+            pl.semaphore_signal(barrier, inc=1, device_id=(me - d, me_tp), device_id_type=MESH)
+
+        @pl.when(me + d < seq)
+        def _():
+            pl.semaphore_signal(barrier, inc=1, device_id=(me + d, me_tp), device_id_type=MESH)
 
     flip[...] = v_ref[...].T
     for ch in range(CHUNKS):
         kv[m, ch, pl.ds(fc, fc), :] = flip[pl.ds(ch * fc, fc), :]
-        kv[m, ch, pl.ds(2 * fc, aug), :] = kaug_ref[...]
-    flip[...] = k_ref[...].T
-    cosine = cos_ref[...]
-    sine = sin_ref[...]
-
-    peers = 1 + tp + (z > 0).astype(jnp.int32) + (z < last_z).astype(jnp.int32)
-    pl.semaphore_wait(barrier, peers)
+    flip_k[...] = k_ref[...].T
+
+    pl.semaphore_wait(
+        barrier, tp - 1 + jnp.minimum(me, span) + jnp.minimum(seq - 1 - me, span)
+    )
+
+    def t_copy(d):
+        return pltpu.make_async_remote_copy(
+            src_ref=tags_ref,
+            dst_ref=tg.at[d - 1],
+            send_sem=t_send.at[d - 1],
+            recv_sem=t_recv.at[d - 1],
+            device_id=(me + d, me_tp),
+            device_id_type=MESH,
+        )
+
+    for d in range(1, span + 1):
+
+        @pl.when(me + d < seq)
+        def _():
+            t_copy(d).start()
 
     def move(src_slot, dst_slot, ch, sem, dev):
         return pltpu.make_async_remote_copy(
@@ -200,7 +201,7 @@
         def _():
             c_copy(lev, ch).start()
 
-    def turned(x, scale):
+    def turned(x, scale, cosine, sine):
         low = x[:HALF].astype(jnp.float32)
         high = x[HALF:].astype(jnp.float32)
         return (
@@ -210,7 +211,12 @@
 
     for ch in range(CHUNKS):
         for hh in range(hc):
-            first, second = turned(flip[pl.ds((ch * hc + hh) * HEAD_DIM, HEAD_DIM), :], 1.0)
+            first, second = turned(
+                flip_k[pl.ds((ch * hc + hh) * HEAD_DIM, HEAD_DIM), :],
+                1.0,
+                cos_ref[...],
+                sin_ref[...],
+            )
             kv[m, ch, pl.ds(hh * HEAD_DIM, HALF), :] = first
             kv[m, ch, pl.ds(hh * HEAD_DIM + HALF, HALF), :] = second
         send_column(0, ch)
@@ -218,7 +224,10 @@
     flip[...] = q_ref[...].T
     for h in range(heads):
         first, second = turned(
-            flip[pl.ds(h * HEAD_DIM, HEAD_DIM), :], math.log2(math.e) / math.sqrt(HEAD_DIM)
+            flip[pl.ds(h * HEAD_DIM, HEAD_DIM), :],
+            math.log2(math.e) / math.sqrt(HEAD_DIM),
+            cos_ref[...],
+            sin_ref[...],
         )
         qx[h, pl.ds(0, HALF), :] = first
         qx[h, pl.ds(HALF, HALF), :] = second
@@ -247,8 +256,42 @@
 
     lax.fori_loop(0, CHUNKS, own_chunk, 0)
 
-    def tile(slot, ch):
-        tags = kv[slot, ch, pl.ds(2 * fc, aug), :]
+    names = tags_ref[pl.ds(aug, 16), :][:1].astype(jnp.float32)
+    opening = names[:, :1]
+    count = jnp.zeros((1, tok), jnp.float32)
+    for d in range(1, span + 1):
+
+        @pl.when(me >= d)
+        def _():
+            t_copy(d).wait_recv()
+
+        @pl.when(me < d)
+        def _():
+            tg[d - 1] = jnp.full(tg.shape[1:], -1.0, tg.dtype)
+
+        earlier = tg[d - 1, pl.ds(aug, 16), :][:1].astype(jnp.float32)
+        count = count + (earlier == opening).astype(jnp.float32)
+    count = jnp.sum(count, axis=1, keepdims=True)
+    place = place_ref[...] + jnp.where(names == opening, count, 0.0)
+    rows = lax.broadcasted_iota(jnp.int32, (HALF, tok), 0).astype(jnp.float32)
+    angles = jnp.exp(rows * (-2.0 * math.log(10000.0) / HEAD_DIM)) * place
+    cosine = jnp.cos(angles)
+    sine = jnp.sin(angles)
+    for h in range(heads):
+        first, second = turned(flip_k[pl.ds(h * HEAD_DIM, HEAD_DIM), :], 1.0, cosine, sine)
+        flip[pl.ds(h * HEAD_DIM, HALF), :] = first
+        flip[pl.ds(h * HEAD_DIM + HALF, HALF), :] = second
+    attn[...] = flip[...].T
+    in_order = table_ref[...][:1, :1] == 0.0
+    for kind, ref in enumerate((attn, v_ref)):
+        lower = ref[pl.ds(0, PAGE), :].astype(jnp.float32) * pad_ref[pl.ds(0, PAGE), :]
+        upper = ref[pl.ds(PAGE, PAGE), :].astype(jnp.float32) * pad_ref[pl.ds(PAGE, PAGE), :]
+        page_ref[0, kind] = jnp.where(in_order, lower, upper).astype(jnp.bfloat16)
+        page_ref[1, kind] = jnp.where(in_order, upper, lower).astype(jnp.bfloat16)
+
+    def tile(lev, mem, ch):
+        slot = lev * LEVEL + mem
+        tags = tg[lev * LEVEL + m - mem - 1, pl.ds(0, aug), :]
         for hh in range(hc):
             h = ch * hc + hh
             keys = jnp.concatenate([kv[slot, ch, pl.ds(hh * HEAD_DIM, HEAD_DIM), :], tags], axis=0)
@@ -285,21 +328,21 @@
 
         @pl.when(a_on)
         def _():
-            tile(nxt * LEVEL + m, ch)
+            tile(nxt, m, ch)
 
         @pl.when(b_in)
         def _():
-            tile(lev * LEVEL + y_mem, ch)
+            tile(lev, y_mem, ch)
 
         @pl.when(c_in)
         def _():
             arrived(lev * LEVEL + core_mem, ch)
-            tile(lev * LEVEL + core_mem, ch)
+            tile(lev, core_mem, ch)
 
         @pl.when(b_in)
         def _():
             arrived(lev * LEVEL + diag_mem, ch)
-            tile(lev * LEVEL + diag_mem, ch)
+            tile(lev, diag_mem, ch)
 
         return carry
 
@@ -392,6 +435,12 @@
     for j in range(1, tp):
         for t in range(nt):
             p_copy(j, t).wait_send()
+    for d in range(1, span + 1):
+
+        @pl.when(me + d < seq)
+        def _():
+            t_copy(d).wait_send()
+
 
     sums = ssq_s[...]
     for j in range(1, tp):
@@ -429,8 +478,9 @@
     device_row = lax.axis_index("seq")
     tok_index = device_row * tok_count + jnp.arange(tok_count, dtype=jnp.int32)
     member = segment_ids[:, None] == jnp.arange(seg_count, dtype=jnp.int32)[None, :]
-    local_first = jnp.min(jnp.where(member, tok_index[:, None], far_index), axis=0)
-    first_tok = lax.pmin(local_first, "seq")
+    offsets = jnp.arange(tok_count, dtype=jnp.int32)
+    local_first = jnp.min(jnp.where(member, offsets[:, None], far_index), axis=0)
+    place = offsets - jnp.sum(jnp.where(member, local_first[None, :], 0), axis=1)
 
     frequency = jnp.exp(
         jnp.arange(HALF, dtype=jnp.float32) * (-2.0 * math.log(10000.0) / HEAD_DIM)
@@ -440,14 +490,20 @@
     aug = max(16, seg_count)
     tags = jnp.where(pad_mask == 1, segment_ids, -1)
     slots = jnp.arange(aug, dtype=jnp.int32)[:, None]
-    kaug = (slots != tags[None, :]).astype(jnp.bfloat16)
+    carried = jnp.concatenate(
+        [
+            (slots != tags[None, :]).astype(jnp.bfloat16),
+            jnp.broadcast_to(segment_ids.astype(jnp.bfloat16)[None, :], (16, tok_count)),
+        ],
+        axis=0,
+    )
     qaug = jnp.where(slots == segment_ids[None, :], masked_score, 0.0).astype(jnp.bfloat16)
-    offsets = jnp.arange(tok_count, dtype=jnp.int32)
     own_visible = (tags[:, None] == segment_ids[None, :]) & (
         offsets[:, None] <= offsets[None, :]
     ) | (offsets[:, None] == offsets[None, :])
     bias = jnp.where(own_visible, 0.0, masked_score).astype(jnp.float32)
 
+    CHUNKS = min(CHUNK_MOST, head_count)
     hc = head_count // CHUNKS
     fc = hc * HEAD_DIM
     nt = feat_count // COLS
@@ -455,15 +511,18 @@
     vm = pl.BlockSpec(memory_space=pltpu.VMEM)
     dma = pltpu.SemaphoreType.DMA
     flops = 4 * head_count * 9 * tok_count * tok_count * HEAD_DIM
-    hidden_out, normed = pl.pallas_call(
+    return pl.pallas_call(
         functools.partial(kernel, seq, tp),
-        out_shape=[jax.ShapeDtypeStruct((tok_count, feat_count), jnp.bfloat16)] * 2,
-        in_specs=[vm] * 10 + [pl.BlockSpec(memory_space=pl.ANY)],
-        out_specs=[vm, vm],
+        out_shape=[jax.ShapeDtypeStruct((tok_count, feat_count), jnp.bfloat16)] * 2
+        + [jax.ShapeDtypeStruct((tok_count // PAGE, 2, PAGE, feat_count), jnp.bfloat16)],
+        in_specs=[vm] * 13 + [pl.BlockSpec(memory_space=pl.ANY)],
+        out_specs=[vm, vm, vm],
         scratch_shapes=[
-            pltpu.VMEM((n_slots, CHUNKS, 2 * fc + aug, tok_count), jnp.bfloat16),
+            pltpu.VMEM((n_slots, CHUNKS, 2 * fc, tok_count), jnp.bfloat16),
             pltpu.VMEM((head_count, HEAD_DIM + aug, tok_count), jnp.bfloat16),
             pltpu.VMEM((feat_count, tok_count), jnp.bfloat16),
+            pltpu.VMEM((feat_count, tok_count), jnp.bfloat16),
+            pltpu.VMEM((reach * LEVEL, aug + 16, tok_count), jnp.bfloat16),
             pltpu.VMEM((tok_count, feat_count), jnp.bfloat16),
             pltpu.VMEM((head_count, 1, tok_count), jnp.float32),
             pltpu.VMEM((head_count, 1, tok_count), jnp.float32),
@@ -484,6 +543,8 @@
             dma((tp - 1, nt)),
             dma((tp - 1,)),
             dma((tp - 1,)),
+            dma((reach * LEVEL,)),
+            dma((reach * LEVEL,)),
         ],
         compiler_params=pltpu.CompilerParams(
             collective_id=0, has_side_effects=True, vmem_limit_bytes=56 * 1024 * 1024
@@ -499,20 +560,14 @@
         norm_gain[None, :],
         cosine,
         sine,
-        kaug,
+        carried,
         qaug,
         bias,
+        place.astype(jnp.float32)[None, :],
+        pad_mask.astype(jnp.float32)[:, None],
+        jnp.broadcast_to(page_table[:1].astype(jnp.float32)[None, :], (8, 128)),
         out_weight,
     )
-
-    position = tok_index - jnp.sum(jnp.where(member, first_tok[None, :], 0), axis=1)
-    k_rot = rotate(key_proj, position, head_count, HEAD_DIM)
-    pad_scale = pad_mask.astype(jnp.bfloat16)[:, None]
-    page_count = tok_count // PAGE
-    stacked = jnp.stack([k_rot * pad_scale, value_proj * pad_scale])
-    stacked = stacked.reshape(2, page_count, PAGE, feat_count).transpose(1, 0, 2, 3)
-    kv_pages = jnp.zeros_like(stacked).at[page_table].set(stacked)
-    return (hidden_out, normed, kv_pages)
 
 
 def solution(mesh):

time: 148 us -> 138 us (0.932)
  blocking collectives: 10.1 us -> 0 us
  Pallas kernels: 118 us -> 122 us
  local copies, waits for them, and re-layouts: 10.1 us -> 6.91 us
  other arithmetic: 9.14 us -> 7.19 us
    pmin x1 -> x0, blocking collectives: 10.1 us -> none  [per_device(): first_tok = lax.pmin(local_first, 'seq')]
    pallas_call x1, Pallas kernels: 118 us -> 122 us  [per_device(): pl.pallas_call(functools.partial(kernel, seq, tp), out_shape=[jax.ShapeDt...]
    transpose x1 -> x0, other arithmetic: 3.48 us -> none  [per_device(): stacked.reshape(2, page_count, PAGE, feat_count).transpose(1, 0, 2, 3)]
    another operation x1 -> x0, local copies, waits for them, and re-layouts: 1.8 us -> none  [per_device(): stacked = jnp.stack([k_rot * pad_scale, value_proj * pad_scale])]
    unnamed x18 -> x7, local copies, waits for them, and re-layouts: 5.33 us -> 4.24 us
where the time goes in v2:
time: 138 us
  Pallas kernels  122 us (88%)
  other arithmetic  7.19 us (5%)
  local copies, waits for them, and re-layouts  6.91 us (5%)
    pallas_call x1, Pallas kernels, per_device(): pl.pallas_call(functools.partial(kernel, seq, tp), out_shape=[jax.ShapeDt...  122 us
    unnamed x7, local copies, waits for them, and re-layouts  4.24 us

profile of v2, /device:TPU:16, one launch (start us, length us, event | category | flops | bytes accessed | tf_op | source)
XLA Modules:
  0.0 137.8 jit_solution(9029548020023548789)
XLA Ops:
  1.3 0.8 select_reduce_fusion.1
  2.1 0.8 select_reduce_fusion
  2.8 0.6 subtract_convert_fusion.place_ref
  3.4 0.8 fusion.4
  4.2 0.6 broadcast_in_dim.93.table_ref
  4.8 1.3 broadcast_in_dim.80.gain_ref
  6.1 0.6 pad_maximum_fusion.tags_ref
  6.7 1.3 select_convert_fusion.qaug_ref
  8.0 0.9 multiply_sine_fusion
  8.9 0.8 copy.13.pad_ref
  9.7 1.5 %fusion.2.bias_ref = f32[256,256]{1,0:T(8,128)} fusion(s32[256]{0:T(256)} %param.15, s32[256]{0:T(256)S(1)} %get-tuple-element.6), kind=kLoop, calls=%fused_computation.4 | loop fusion | flops 393216 | bytes 264192 | tf_op jit(solution)/shard_map/jit(_where)/select_n | solution.py:504
  11.1 122.3 %shard_map.112 = (bf16[256,1536]{1,0:T(8,128)(2,1)}, bf16[256,1536]{1,0:T(8,128)(2,1)}, bf16[2,2,128,1536]{3,2,1,0:T(8,128)(2,1)}) custom-call(bf16[256,1536]{1,0:T(8,128)(2,1)} %q_ref.1, bf16[256,1536]{1,0:T(8,128)(2,1)} %k_ref.1, bf16[256,1536]{1,0:T(8,128)(2,1)} %v_ref.1, bf16[256,1536]{1,0:T(8,128)(2,1)} %hid_ref.1, ...), custom_call_target="tpu_custom_call" | custom-call | flops 3623878656 | bytes 16777216 | tf_op jit(solution)/shard_map/pallas_call | solution.py:514
  133.5 0.0 copy-start.1
  133.5 0.0 copy-start
  133.5 2.2 %copy.17 = bf16[256,1536]{1,0:T(8,128)(2,1)} copy(bf16[256,1536]{1,0:T(8,128)(2,1)} %get-tuple-element.11) | data formatting | bytes 1572864
  135.7 0.0 copy-done.1
  135.7 0.9 copy.18
  136.6 0.0 copy-done
  136.6 1.1 copy.19
  (4 shorter events, 0.0 us)
Async XLA Ops:
  133.5 2.2 %copy-start.1 = (bf16[256,1536]{1,0:T(8,128)(2,1)S(1)}, bf16[256,1536]{1,0:T(8,128)(2,1)}, u32[]{:S(2)}) copy-start(bf16[256,1536]{1,0:T(8,128)(2,1)} %get-tuple-element.12) | copy-start | bytes 2359300
  133.5 3.1 %copy-start = (bf16[2,2,128,1536]{3,2,1,0:T(8,128)(2,1)S(1)}, bf16[2,2,128,1536]{3,2,1,0:T(8,128)(2,1)}, u32[]{:S(2)}) copy-start(bf16[2,2,128,1536]{3,2,1,0:T(8,128)(2,1)} %get-tuple-element.13) | copy-start | bytes 4718596

commit v3 on v2

--- a/solution.py
+++ b/solution.py
@@ -14,6 +14,7 @@
 PAGE = 128
 LEVEL = 4
 CHUNK_MOST = 8
+LAG = 2
 COLS = 384
 
 far_index = 1073741824
@@ -53,8 +54,8 @@
     acc,
     w_s,
     own_p,
-    sbuf,
-    rbuf,
+    w_far,
+    a_far,
     ssq_s,
     ssq_r,
     w_sem,
@@ -63,8 +64,12 @@
     c_send,
     d_send,
     recv,
-    p_send,
-    p_recv,
+    a_send,
+    a_recv,
+    wf_send,
+    wf_recv,
+    wc_send,
+    wc_recv,
     s_send,
     s_recv,
     t_send,
@@ -92,8 +97,11 @@
     last_z = seq // LEVEL - 1
     span = reach * LEVEL
 
-    w_copy = pltpu.make_async_copy(w_hbm, w_s, w_sem)
+    w_copy = pltpu.make_async_copy(
+        w_hbm.at[:, pl.ds(pl.multiple_of(me_tp * feat, 128), feat)], w_s, w_sem
+    )
     w_copy.start()
+    half = feat // 2
 
     barrier = pltpu.get_barrier_semaphore()
     for j in range(1, tp):
@@ -134,6 +142,46 @@
         @pl.when(me + d < seq)
         def _():
             t_copy(d).start()
+
+    def w_copy_far(j):
+        to = (me_tp + j) % tp
+        rows = pl.ds(pl.multiple_of(mc * half, 16), half)
+        return pltpu.make_async_remote_copy(
+            src_ref=w_hbm.at[rows, pl.ds(pl.multiple_of(to * feat, 128), feat)],
+            dst_ref=w_far.at[j - 1, rows, :],
+            send_sem=wf_send.at[j - 1],
+            recv_sem=wf_recv.at[j - 1],
+            device_id=(me, to),
+            device_id_type=MESH,
+        )
+
+    def w_between(j, core):
+        rows = pl.ds(pl.multiple_of(core * half, 16), half)
+        return pltpu.make_async_remote_copy(
+            src_ref=w_far.at[j - 1, rows, :],
+            dst_ref=w_far.at[j - 1, rows, :],
+            send_sem=wc_send.at[j - 1],
+            recv_sem=wc_recv.at[j - 1],
+            device_id=(core_dev, me_tp),
+            device_id_type=MESH,
+        )
+
+    def w_copy_core(j):
+        return w_between(j, mc)
+
+    def w_core_arrived(j):
+        w_between(j, 1 - mc).wait_recv()
+
+    def a_copy(j, ch):
+        rows = pl.ds(pl.multiple_of(ch * fc, 16), fc)
+        return pltpu.make_async_remote_copy(
+            src_ref=flip.at[rows, :],
+            dst_ref=a_far.at[j - 1, rows, :],
+            send_sem=a_send.at[j - 1, ch],
+            recv_sem=a_recv.at[j - 1, ch],
+            device_id=(me, (me_tp + j) % tp),
+            device_id_type=MESH,
+        )
 
     def move(src_slot, dst_slot, ch, sem, dev):
         return pltpu.make_async_remote_copy(
@@ -220,6 +268,8 @@
             kv[m, ch, pl.ds(hh * HEAD_DIM, HALF), :] = first
             kv[m, ch, pl.ds(hh * HEAD_DIM + HALF, HALF), :] = second
         send_column(0, ch)
+    for j in range(1, tp):
+        w_copy_far(j).start()
 
     flip[...] = q_ref[...].T
     for h in range(heads):
@@ -308,86 +358,93 @@
                 preferred_element_type=jnp.float32,
             )
 
+    def others(lev, ch):
+        b_in = b_on(lev)
+
+        @pl.when(b_in)
+        def _():
+            arrived(lev * LEVEL + y_mem, ch)
+            d_copy(lev, ch).start()
+            tile(lev, y_mem, ch)
+
+        @pl.when(cr_on(lev))
+        def _():
+            arrived(lev * LEVEL + core_mem, ch)
+            tile(lev, core_mem, ch)
+
+        @pl.when(b_in)
+        def _():
+            arrived(lev * LEVEL + diag_mem, ch)
+            tile(lev, diag_mem, ch)
+
+    def finish(ch):
+        for hh in range(hc):
+            h = ch * hc + hh
+            rows = pl.ds(pl.multiple_of(h * HEAD_DIM, HEAD_DIM), HEAD_DIM)
+            flip[rows, :] = (acc[h] / l_s[h]).astype(jnp.bfloat16)
+        for j in range(1, tp):
+            a_copy(j, ch).start()
+
+    late = (reach - 1) * CHUNKS + LAG
+
     def step(g, carry):
         lev = g // CHUNKS
         ch = g % CHUNKS
         nxt = lev + 1
         a_on = (nxt <= reach) & (z - nxt >= 0)
-        b_in = b_on(lev)
-        c_in = cr_on(lev)
 
         @pl.when(a_on)
         def _():
             arrived(nxt * LEVEL + m, ch)
             send_column(nxt, ch)
-
-        @pl.when(b_in)
-        def _():
-            arrived(lev * LEVEL + y_mem, ch)
-            d_copy(lev, ch).start()
-
-        @pl.when(a_on)
-        def _():
             tile(nxt, m, ch)
 
-        @pl.when(b_in)
-        def _():
-            tile(lev, y_mem, ch)
-
-        @pl.when(c_in)
-        def _():
-            arrived(lev * LEVEL + core_mem, ch)
-            tile(lev, core_mem, ch)
-
-        @pl.when(b_in)
-        def _():
-            arrived(lev * LEVEL + diag_mem, ch)
-            tile(lev, diag_mem, ch)
+        @pl.when(lev < reach)
+        def _():
+            others(lev, ch)
+
+        @pl.when(g >= late)
+        def _():
+            others(reach, g - late)
+            finish(g - late)
+
+        @pl.when(g == reach * CHUNKS - 1)
+        def _():
+            for j in range(1, tp):
+                w_copy_far(j).wait_recv()
+                w_copy_core(j).start()
 
         return carry
 
-    lax.fori_loop(0, (reach + 1) * CHUNKS, step, 0)
-
-    for h in range(heads):
-        flip[pl.ds(h * HEAD_DIM, HEAD_DIM), :] = (acc[h] / l_s[h]).astype(jnp.bfloat16)
+    lax.fori_loop(0, reach * CHUNKS + LAG, step, 0)
+
     w_copy.wait()
     attn[...] = flip[...].T
 
-    def p_copy(j, t):
-        return pltpu.make_async_remote_copy(
-            src_ref=sbuf.at[j - 1, t],
-            dst_ref=rbuf.at[j - 1, t],
-            send_sem=p_send.at[j - 1, t],
-            recv_sem=p_recv.at[j - 1, t],
-            device_id=(me, (me_tp + j) % tp),
-            device_id_type=MESH,
-        )
-
-    def product(to, t):
-        start = pl.multiple_of(to * feat + t * COLS, COLS)
-        return jnp.dot(attn[...], w_s[:, pl.ds(start, COLS)], preferred_element_type=jnp.float32)
-
+    def keep(t, carry):
+        cols = pl.ds(pl.multiple_of(t * COLS, COLS), COLS)
+        own_p[t] = jnp.dot(attn[...], w_s[:, cols], preferred_element_type=jnp.float32)
+        return carry
+
+    lax.fori_loop(0, nt, keep, 0)
     for j in range(1, tp):
-
-        def give(t, carry):
-            sbuf[j - 1, t] = product((me_tp + j) % tp, t).astype(jnp.bfloat16)
-            p_copy(j, t).start()
+        for ch in range(CHUNKS):
+            a_copy(j, ch).wait_recv()
+        w_core_arrived(j)
+        attn[...] = a_far[j - 1].T
+
+        def more(t, carry):
+            cols = pl.ds(pl.multiple_of(t * COLS, COLS), COLS)
+            own_p[t] = own_p[t] + jnp.dot(
+                attn[...], w_far[j - 1, :, cols], preferred_element_type=jnp.float32
+            )
             return carry
 
-        lax.fori_loop(0, nt, give, 0)
-
-    def keep(t, carry):
-        own_p[t] = product(me_tp, t)
-        return carry
-
-    lax.fori_loop(0, nt, keep, 0)
+        lax.fori_loop(0, nt, more, 0)
 
     square = jnp.zeros((tok, 1), jnp.float32)
     for t in range(nt):
         total = own_p[t]
-        for j in range(1, tp):
-            p_copy(j, t).wait_recv()
-            total = total + rbuf[j - 1, t].astype(jnp.float32)
         cols = pl.ds(t * COLS, COLS)
         fresh = (hid_ref[:, cols].astype(jnp.float32) + total).astype(jnp.bfloat16)
         out_ref[:, cols] = fresh
@@ -433,8 +490,10 @@
 
     lax.fori_loop(0, (reach + 1) * CHUNKS, drain, 0)
     for j in range(1, tp):
-        for t in range(nt):
-            p_copy(j, t).wait_send()
+        for ch in range(CHUNKS):
+            a_copy(j, ch).wait_send()
+        w_copy_far(j).wait_send()
+        w_copy_core(j).wait_send()
     for d in range(1, span + 1):
 
         @pl.when(me + d < seq)
@@ -527,10 +586,10 @@
             pltpu.VMEM((head_count, 1, tok_count), jnp.float32),
             pltpu.VMEM((head_count, 1, tok_count), jnp.float32),
             pltpu.VMEM((head_count, HEAD_DIM, tok_count), jnp.float32),
-            pltpu.VMEM(out_weight.shape, jnp.bfloat16),
+            pltpu.VMEM((feat_count, feat_count), jnp.bfloat16),
             pltpu.VMEM((nt, tok_count, COLS), jnp.float32),
-            pltpu.VMEM((tp - 1, nt, tok_count, COLS), jnp.bfloat16),
-            pltpu.VMEM((tp - 1, nt, tok_count, COLS), jnp.bfloat16),
+            pltpu.VMEM((tp - 1, feat_count, feat_count), jnp.bfloat16),
+            pltpu.VMEM((tp - 1, feat_count, tok_count), jnp.bfloat16),
             pltpu.VMEM((8, tok_count), jnp.float32),
             pltpu.VMEM((tp - 1, 8, tok_count), jnp.float32),
             dma,
@@ -539,8 +598,12 @@
             dma((reach + 1, CHUNKS)),
             dma((reach + 1, CHUNKS)),
             dma((n_slots, CHUNKS)),
-            dma((tp - 1, nt)),
-            dma((tp - 1, nt)),
+            dma((tp - 1, CHUNKS)),
+            dma((tp - 1, CHUNKS)),
+            dma((tp - 1,)),
+            dma((tp - 1,)),
+            dma((tp - 1,)),
+            dma((tp - 1,)),
             dma((tp - 1,)),
             dma((tp - 1,)),
             dma((reach * LEVEL,)),

time: 138 us -> 122 us (0.88)
  Pallas kernels: 122 us -> 106 us
    pallas_call x1, Pallas kernels: 122 us -> 106 us  [per_device(): pl.pallas_call(functools.partial(kernel, seq, tp), out_shape=[jax.ShapeDt...]
where the time goes in v3:
time: 122 us
  Pallas kernels  106 us (87%)
  other arithmetic  7.19 us (6%)
  local copies, waits for them, and re-layouts  6.91 us (6%)
  between operations  1.31 us (1%)
    pallas_call x1, Pallas kernels, per_device(): pl.pallas_call(functools.partial(kernel, seq, tp), out_shape=[jax.ShapeDt...  106 us
    unnamed x7, local copies, waits for them, and re-layouts  4.24 us

profile of v3, /device:TPU:16, one launch (start us, length us, event | category | flops | bytes accessed | tf_op | source)
XLA Modules:
  0.0 121.8 jit_solution(17841092199793990896)
XLA Ops:
  1.3 0.8 select_reduce_fusion.1
  2.1 0.8 select_reduce_fusion
  2.8 0.6 subtract_convert_fusion.place_ref
  3.4 0.8 fusion.4
  4.2 0.6 broadcast_in_dim.93.table_ref
  4.8 1.3 %broadcast_in_dim.80.gain_ref = bf16[1,1536]{1,0:T(2,128)(2,1)} reshape(bf16[1536]{0:T(1024)(128)(2,1)} %param.14) | data formatting | bytes 6144 | tf_op jit(solution)/shard_map/broadcast_in_dim | solution.py:623
  6.1 0.6 pad_maximum_fusion.tags_ref
  6.7 1.3 %select_convert_fusion.qaug_ref = bf16[16,256]{1,0:T(8,128)(2,1)} fusion(s32[256]{0:T(256)} %param.15), kind=kLoop, calls=%fused_computation.8 | loop fusion | flops 12288 | bytes 9216 | tf_op jit(solution)/shard_map/convert_element_type | solution.py:559
  8.0 0.9 multiply_sine_fusion
  8.9 0.8 copy.13.pad_ref
  9.7 1.5 %fusion.2.bias_ref = f32[256,256]{1,0:T(8,128)} fusion(s32[256]{0:T(256)} %param.15, s32[256]{0:T(256)S(1)} %get-tuple-element.6), kind=kLoop, calls=%fused_computation.4 | loop fusion | flops 393216 | bytes 264192 | tf_op jit(solution)/shard_map/jit(_where)/select_n | solution.py:563
  11.1 106.4 %shard_map.112 = (bf16[256,1536]{1,0:T(8,128)(2,1)}, bf16[256,1536]{1,0:T(8,128)(2,1)}, bf16[2,2,128,1536]{3,2,1,0:T(8,128)(2,1)}) custom-call(bf16[256,1536]{1,0:T(8,128)(2,1)} %q_ref.1, bf16[256,1536]{1,0:T(8,128)(2,1)} %k_ref.1, bf16[256,1536]{1,0:T(8,128)(2,1)} %v_ref.1, bf16[256,1536]{1,0:T(8,128)(2,1)} %hid_ref.1, ...), custom_call_target="tpu_custom_call" | custom-call | flops 3623878656 | bytes 16777216 | tf_op jit(solution)/shard_map/pallas_call | solution.py:573
  117.5 0.0 copy-start.1
  117.6 0.0 copy-start
  117.6 2.2 %copy.17 = bf16[256,1536]{1,0:T(8,128)(2,1)} copy(bf16[256,1536]{1,0:T(8,128)(2,1)} %get-tuple-element.11) | data formatting | bytes 1572864
  119.8 0.0 copy-done.1
  119.8 0.9 copy.18
  120.7 0.0 copy-done
  120.7 1.1 copy.19
  (4 shorter events, 0.0 us)
Async XLA Ops:
  117.5 2.2 %copy-start.1 = (bf16[256,1536]{1,0:T(8,128)(2,1)S(1)}, bf16[256,1536]{1,0:T(8,128)(2,1)}, u32[]{:S(2)}) copy-start(bf16[256,1536]{1,0:T(8,128)(2,1)} %get-tuple-element.12) | copy-start | bytes 2359300
  117.6 3.1 %copy-start = (bf16[2,2,128,1536]{3,2,1,0:T(8,128)(2,1)S(1)}, bf16[2,2,128,1536]{3,2,1,0:T(8,128)(2,1)}, u32[]{:S(2)}) copy-start(bf16[2,2,128,1536]{3,2,1,0:T(8,128)(2,1)} %get-tuple-element.13) | copy-start | bytes 4718596
